TPU v7x, 32 devices: a whole 2x2x4 slice. The times are simulated.
32 devices in a mesh: row: 8 (over y, x, core), col: 4 (over z).
Axes of the slice: x: 2, y: 2, z: 4, core: 2. Of those that a mesh axis runs over, the one named last changes fastest.
Arguments:
- matrix: float32 [5120, 8192], P('row', 'col'), may hold values from -100 to 100
- pivots: int32 [256], replicated, may hold values from 0 to 8191, as said below
- sketch: float32 [264, 8192], P(None, ('col', 'row')), may hold values from -6 to 6
Outputs:
- upper_rows: float32 [256, 8192], P(None, ('col', 'row'))
- trailing: float32 [5120, 8192], P('row', 'col')
- new_sketch: float32 [264, 8192], P(None, ('col', 'row'))
Inputs may be any that keep to these rules, and one draw needn't show every extreme that they name: `pivots`: 256 distinct column indices.
All inputs are finite; a program needn't handle non-finite values.
Results may differ from a plain program's by a relative error of at most 0.0003.
Values sent between devices are 32-bit elements; how exact they have to be, the bound alone decides.
A program may use at most 128 MiB of HBM per device.

v0:
```python
import jax
import jax.numpy as jnp
from jax import lax
from jax.sharding import PartitionSpec as P

sentinel_value = 1 << 30
highest = lax.Precision.HIGHEST
contract = (((0,), (0,)), ((), ()))


def inner(left, right):
    return lax.dot_general(
        left, right, contract, precision=highest, preferred_element_type=jnp.float32
    )


def pairing(pivots):
    panel_cols = pivots.shape[0]
    positions = jnp.arange(panel_cols, dtype=jnp.int32)
    present = jnp.any(pivots[None, :] == positions[:, None], axis=1)
    displaced = jnp.sort(jnp.where(present, sentinel_value, positions))
    vacated = jnp.sort(jnp.where(pivots >= panel_cols, pivots, sentinel_value))
    return (vacated, displaced)


def collect(source, offset, wanted):
    columns = source.shape[1]
    offsets = wanted - offset
    holding = (offsets >= 0) & (offsets < columns)
    picked = jnp.take(source, jnp.clip(offsets, 0, columns - 1), axis=1)
    return jnp.where(holding[None, :], picked, 0.0)


def arrange(source, offset, fronts, former, vacated, displaced):
    columns = source.shape[1]
    panel_cols = fronts.shape[1]
    usable = (vacated >= offset) & (vacated < offset + columns)
    target = jnp.where(usable, vacated - offset, columns)
    anchor = jnp.clip(displaced, 0, panel_cols - 1)
    arranged = source.at[:, target].set(jnp.take(former, anchor, axis=1), mode="drop")
    global_pos = offset + jnp.arange(columns, dtype=jnp.int32)
    leading = jnp.take(fronts, jnp.clip(global_pos, 0, panel_cols - 1), axis=1)
    return jnp.where(global_pos[None, :] < panel_cols, leading, arranged)


def per_device(matrix, pivots, sketch):
    col_index = lax.axis_index("col")
    row_index = lax.axis_index("row")
    columns = matrix.shape[1]
    panel_cols = pivots.shape[0]
    pieces = sketch.shape[1]
    vacated, displaced = pairing(pivots)
    firsts = jnp.arange(panel_cols, dtype=jnp.int32)
    offset = col_index * columns
    panel, former = lax.psum(
        (collect(matrix, offset, pivots), collect(matrix, offset, firsts)), "col"
    )
    sketch_offset = offset + row_index * pieces
    fronts_sketch, former_sketch = lax.psum(
        (collect(sketch, sketch_offset, pivots), collect(sketch, sketch_offset, firsts)),
        ("row", "col"),
    )
    permuted = arrange(matrix, offset, panel, former, vacated, displaced)
    moved = arrange(sketch, sketch_offset, fronts_sketch, former_sketch, vacated, displaced)
    local_gram = inner(panel, panel)
    product = inner(panel, permuted)
    gram_total, summed = lax.psum((local_gram, product), "row")
    lower_factor = jnp.linalg.cholesky(gram_total)
    upper_full = lax.linalg.triangular_solve(lower_factor, summed, left_side=True, lower=True)
    upper_share = lax.dynamic_slice_in_dim(upper_full, row_index * pieces, pieces, 1)
    basis = lax.linalg.triangular_solve(
        lower_factor, panel, left_side=False, lower=True, transpose_a=True
    )
    trailing = permuted - jnp.dot(
        basis, upper_full, precision=highest, preferred_element_type=jnp.float32
    )
    solved = lax.linalg.triangular_solve(
        lower_factor, upper_share, left_side=True, lower=True, transpose_a=True
    )
    new_sketch = moved - jnp.dot(
        fronts_sketch, solved, precision=highest, preferred_element_type=jnp.float32
    )
    return (upper_share, trailing, new_sketch)


def solution(mesh):
    return jax.shard_map(
        per_device,
        mesh=mesh,
        in_specs=(P("row", "col"), P(), P(None, ("col", "row"))),
        out_specs=(P(None, ("col", "row")), P("row", "col"), P(None, ("col", "row"))),
        check_vma=False,
    )
```

profile of v0, /device:TPU:0, one launch (start us, length us, event | category | flops | bytes accessed | tf_op | source)
XLA Modules:
  0.0 374.7 jit_solution(6084200813679883449)
XLA Ops:
  7.3 5.9 %copy.30 = f32[640,2048]{0,1:T(8,128)} copy(f32[640,2048]{1,0:T(8,128)} %param.7) | data formatting | bytes 10485760 | tf_op args[0]
  13.2 3.8 %gather_fusion.1 = f32[256,640]{1,0:T(8,128)S(1)} fusion(f32[640,2048]{0,1:T(8,128)} %copy.30, s32[1024]{0:T(1024)S(1)} %pad_clamp_fusion.5), kind=kCustom, calls=%fused_computation.clone | custom fusion | bytes 1311744 | tf_op jit(solution)/shard_map/jit(_take)/gather | solution.py:30
  17.2 3.8 %gather_fusion.2 = f32[256,640]{1,0:T(8,128)S(1)} fusion(f32[640,2048]{0,1:T(8,128)} %copy.30, s32[1024]{0:T(1024)S(1)} %pad_clamp_fusion.4), kind=kCustom, calls=%fused_computation.2.clone | custom fusion | bytes 1311744 | tf_op jit(solution)/shard_map/jit(_take)/gather | solution.py:30
  21.3 0.9 bitcast_select_fusion.3
  22.2 0.9 bitcast_select_fusion.2
  23.4 1.0 gather_fusion.3
  24.4 1.0 gather_fusion.5
  25.4 0.9 bitcast_select_fusion.5
  26.3 0.9 bitcast_select_fusion.4
  27.5 3.2 sort.28
  30.7 3.2 sort.21
  33.9 52.6 %all-reduce.12.cloned.1.call-done = (f32[640,256]{1,0:T(8,128)}, f32[640,256]{1,0:T(8,128)}) async-done(((f32[640,256]{1,0:T(8,128)}, f32[640,256]{1,0:T(8,128)}), (f32[640,256]{1,0:T(8,128)}, f32[640,256]{1,0:T(8,128)})) %all-reduce.12.cloned.1.call-update) | async-done | bytes 1310736 | tf_op jit(solution)/shard_map/psum | solution.py:55
  86.4 1.3 copy.38
  87.8 7.2 %scatter_custom_fusion = f32[640,2048]{0,1:T(8,128)} fusion(f32[640,2048]{0,1:T(8,128)} %copy.30, s32[256]{0:T(256)S(1)} %get-tuple-element.44, f32[]{:T(128)} %constant.153.clone.1, pred[256]{0:T(512)(128)(4,1)S(1)} %compare_and_fusion.8, f32[640,256]{0,1:T(8,128)S(1)} %copy.38, s32[1024]{0:T(1024)S(1)} %pad_clamp_fusion.3), kind=kCustom, calls=%fused_computation.30 | custom fusion | flops 163840 | bytes 5903360 | tf_op jit(solution)/shard_map/scatter | solution.py:40
  95.0 6.0 %copy.40 = f32[640,2048]{1,0:T(8,128)} copy(f32[640,2048]{0,1:T(8,128)} %scatter_custom_fusion) | data formatting | bytes 10485760 | tf_op jit(solution)/shard_map/scatter | solution.py:40
  101.2 9.3 %gather_fusion = f32[2048,640]{1,0:T(8,128)} fusion(f32[640,256]{0,1:T(8,128)S(1)} %copy.34, s32[2048]{0:T(1024)S(1)} %broadcast_clamp_fusion), kind=kCustom, calls=%fused_computation.6 | custom fusion | bytes 10493952 | tf_op jit(solution)/shard_map/jit(_take)/gather | solution.py:42
  110.5 6.1 %copy.35 = f32[2048,640]{0,1:T(8,128)} copy(f32[2048,640]{1,0:T(8,128)} %gather_fusion) | data formatting | bytes 10485760 | tf_op jit(solution)/shard_map/jit(_take)/gather | solution.py:42
  116.6 9.2 %fusion = f32[256,2048]{1,0:T(8,128)} fusion(f32[640,256]{1,0:T(8,128)S(1)} %copy-done.1, f32[640,2048]{1,0:T(8,128)} %copy.40, f32[2048,640]{0,1:T(8,128)} %copy.35, pred[2048]{0:T(1024)(128)(4,1)S(1)} %get-tuple-element.58, pred[2048]{0:T(1024)(128)(4,1)S(1)} %get-tuple-element.57), kind=kOutput, calls=%fused_computation.18 | convolution fusion | flops 4029153280 | bytes 13242368 | tf_op jit(solution)/shard_map/dot_general | solution.py:12
  125.8 1.9 fusion.44
  127.8 93.2 %all-reduce.8.cloned.1.call-done = (f32[264,256]{0,1:T(8,128)}, f32[264,256]{0,1:T(8,128)}) async-done(((f32[264,256]{0,1:T(8,128)}, f32[264,256]{0,1:T(8,128)}), (f32[264,256]{0,1:T(8,128)}, f32[264,256]{0,1:T(8,128)})) %all-reduce.8.cloned.1.call-update) | async-done | bytes 540688 | tf_op jit(solution)/shard_map/psum | solution.py:59
  221.0 6.3 %scatter_custom_fusion.1 = f32[264,256]{0,1:T(8,128)S(1)} fusion(f32[264,256]{0,1:T(8,128)S(1)} %copy.41, s32[256]{0:T(256)S(1)} %get-tuple-element.43, f32[]{:T(128)} %constant.153.clone.1, pred[256]{0:T(512)(128)(4,1)S(1)} %compare_and_fusion.8, f32[264,256]{0,1:T(8,128)} %get-tuple-element.28, s32[1024]{0:T(1024)S(1)} %pad_clamp_fusion.3), kind=kCustom, calls=%fused_computation.34 | custom fusion | flops 67584 | bytes 545284 | tf_op jit(solution)/shard_map/scatter | solution.py:40
  227.5 2.1 gather_fusion.4
  229.8 57.6 %all-reduce.10.cloned.1.call-done = (f32[256,2048]{1,0:T(8,128)}, f32[256,256]{0,1:T(8,128)}) async-done(((f32[256,2048]{1,0:T(8,128)}, f32[256,256]{0,1:T(8,128)}), (f32[256,2048]{1,0:T(8,128)}, f32[256,256]{0,1:T(8,128)})) %all-reduce.10.cloned.1.call-update) | async-done | bytes 2359312 | tf_op jit(solution)/shard_map/psum | solution.py:67
  287.3 1.1 copy.33
  288.4 1.0 fusion.18
  289.4 11.7 %cholesky.50 = f32[128,128]{1,0:T(8,128)S(1)} custom-call(f32[128,128]{1,0:T(8,128)S(1)} %cholesky.118), custom_call_target="Cholesky" | custom-call | tf_op jit(solution)/shard_map/jit(cholesky)/cholesky | solution.py:68
  301.2 9.8 %custom-call.18 = f32[1,128,128]{1,2,0:T(8,128)S(1)} custom-call(f32[1,128,128]{2,1,0:T(8,128)S(1)} %get-tuple-element.42), custom_call_target="InvertDiagBlocksLowerTriangular" | custom-call | tf_op jit(solution)/shard_map/jit(cholesky)/cholesky | solution.py:68
  311.2 0.3 convolution_subtract_fusion.5
  311.5 11.7 %cholesky.105 = f32[128,128]{1,0:T(8,128)S(1)} custom-call(f32[128,128]{1,0:T(8,128)S(1)} %convolution_subtract_fusion.5), custom_call_target="Cholesky" | custom-call | tf_op jit(solution)/shard_map/jit(cholesky)/cholesky | solution.py:68
  323.2 0.6 compare_reduce_fusion.1
  323.9 0.6 compare_reduce_fusion
  325.9 4.2 %while.1 = (s32[]{:T(128)}, f32[256,256]{1,0:T(8,128)S(1)}, s32[2,2]{1,0:T(2,128)S(1)}, f32[2,128,128]{2,1,0:T(8,128)S(1)}, s32[]{:T(128)}) while((s32[]{:T(128)}, f32[256,256]{1,0:T(8,128)S(1)}, s32[2,2]{1,0:T(2,128)S(1)}, f32[2,128,128]{2,1,0:T(8,128)S(1)}, s32[]{:T(128)}) %tuple.41), condition=%wide.while_cond, body=%wide.while_body.sunk | while | flops 2 | bytes 131189 | solution.py:69
  326.1 0.6 fusion.58
  326.7 1.4 bitcast_dynamic-update-slice_fusion.2
  328.1 0.6 fusion.58
  328.7 1.4 bitcast_dynamic-update-slice_fusion.2
  330.1 19.7 %custom-call.19 = f32[2,128,128]{1,2,0:T(8,128)S(1)} custom-call(f32[2,128,128]{2,1,0:T(8,128)S(1)} %get-tuple-element.18), custom_call_target="InvertDiagBlocksLowerTriangular" | custom-call | tf_op jit(solution)/shard_map/triangular_solve | solution.py:69
  349.8 0.5 fusion.10
  350.3 2.3 fusion.1
  352.6 2.4 convolution_subtract_fusion.1
  355.0 1.1 fusion.29
  356.0 0.7 convolution_subtract_fusion.2
  356.7 0.5 fusion.28
  357.3 8.5 %convolution_subtract_fusion = f32[640,2048]{1,0:T(8,128)} fusion(f32[128,2048]{1,0:T(8,128)S(1)} %fusion.29, f32[128,2048]{1,0:T(8,128)S(1)} %fusion.1, f32[640,2048]{1,0:T(8,128)S(1)} %bitcast.65, f32[2048,640]{0,1:T(8,128)} %copy.35, pred[2048]{0:T(1024)(128)(4,1)S(1)} %get-tuple-element.58, pred[2048]{0:T(1024)(128)(4,1)S(1)} %get-tuple-element.57, ...), kind=kOutput, calls=%fused_computation.13 | convolution fusion | flops 4031152128 | bytes 18485248 | tf_op jit(solution)/shard_map/dot_general | solution.py:74
  365.8 0.3 fusion.22
  366.1 0.3 convolution_subtract_fusion.4
  366.4 0.3 fusion.27
  366.7 1.5 convolution_subtract_fusion.3
  (62 shorter events, 2.1 us)
Async XLA Ops:
  7.2 79.3 %all-reduce.12.cloned.1.call-start = ((), (), s32[]{:S(2)}) async-start(), calls=%async_computation.2 | async-start | bytes 2621440 | tf_op jit(solution)/shard_map/psum | solution.py:55
  7.2 5.9 %copy-start.4 = (s32[256]{0:T(256)S(1)}, s32[256]{0:T(256)}, u32[]{:S(2)}) copy-start(s32[256]{0:T(256)} %param.8) | copy-start | bytes 3076
  17.2 6.0 %copy-start.3 = (f32[264,256]{1,0:T(8,128)S(1)}, f32[264,256]{1,0:T(8,128)}, u32[]{:S(2)}) copy-start(f32[264,256]{1,0:T(8,128)} %param.9) | copy-start | bytes 811012
  23.2 197.9 %all-reduce.8.cloned.1.call-start = ((), (), s32[]{:S(2)}) async-start(), calls=%async_computation | async-start | bytes 1572864 | tf_op jit(solution)/shard_map/psum | solution.py:59
  27.2 260.1 %all-reduce.10.cloned.1.call-start = ((), (), s32[]{:S(2)}) async-start(), calls=%async_computation.1 | async-start | bytes 4718592 | tf_op jit(solution)/shard_map/psum | solution.py:67
  95.0 6.0 %copy-start.1 = (f32[640,256]{1,0:T(8,128)S(1)}, f32[640,256]{1,0:T(8,128)}, u32[]{:S(2)}) copy-start(f32[640,256]{1,0:T(8,128)} %get-tuple-element.31) | copy-start | bytes 1966084
  325.8 31.4 %slice-start = ((s8[5242880]{0:T(1024)(128)(4,1)}), s8[1048576]{0:T(1024)(128)(4,1)S(1)}, s32[]{:S(2)}) async-start(s8[5242880]{0:T(1024)(128)(4,1)} %bitcast.64), calls=%async_computation.3 | async-start | bytes 2097152
  352.6 4.7 %slice-start.1 = ((s8[5242880]{0:T(1024)(128)(4,1)}), s8[4194304]{0:T(1024)(128)(4,1)S(1)}, s32[]{:S(2)}) async-start(s8[5242880]{0:T(1024)(128)(4,1)} %bitcast.64), calls=%async_computation.4 | async-start | bytes 8388608
  357.3 8.8 %copy-start.2 = (f32[256,256]{1,0:T(8,128)}, f32[256,256]{1,0:T(8,128)S(1)}, u32[]{:S(2)}) copy-start(f32[256,256]{1,0:T(8,128)S(1)} %fusion.14) | copy-start | bytes 786436
  357.3 9.4 %copy-start = (f32[264,256]{0,1:T(8,128)S(1)}, f32[264,256]{0,1:T(8,128)}, u32[]{:S(2)}) copy-start(f32[264,256]{0,1:T(8,128)} %get-tuple-element.27) | copy-start | bytes 811012
Sparse Core Ops, SparseCore 0:
  23.3 63.1 all-reduce.11
  91.8 129.1 all-reduce.7
  225.3 62.0 all-reduce.9
where the time goes:
time: 375 us
  waiting for transfers between devices  203 us (54%)
  other arithmetic  79.1 us (21%)
  local copies, waits for them, and re-layouts  46.5 us (12%)
  matrix products  29.8 us (8%)
  between operations  15.5 us (4%)
    psum x1, waiting for transfers between devices, per_device(): lax.psum((collect(sketch, sketch_offset, pivots), collect(sketch, sketch_...  93.2 us
    psum x1, waiting for transfers between devices, per_device(): gram_total, summed = lax.psum((local_gram, product), 'row')  57.6 us
    psum x1, waiting for transfers between devices, per_device(): lax.psum((collect(matrix, offset, pivots), collect(matrix, offset, firsts...  52.6 us
    another operation x7, other arithmetic, per_device(): lower_factor = jnp.linalg.cholesky(gram_total)  34.6 us
    another operation x4, other arithmetic, per_device(): lax.linalg.triangular_solve(lower_factor, summed, left_side=True, lower=T...  19.7 us
    gather x4, local copies, waits for them, and re-layouts, arrange(): leading = jnp.take(fronts, jnp.clip(global_pos, 0, panel_cols - 1), axis=1)  17.6 us
    scatter x2, other arithmetic, arrange(): source.at[:, target].set(jnp.take(former, anchor, axis=1), mode='drop')  13.6 us
    dot_general x2, matrix products, inner(): lax.dot_general(left, right, contract, precision=highest, preferred_eleme...  11.1 us
  transfers between devices with their start and end apart: 3, of which 3 were waited for; matrix products, arithmetic and copies ran while one was open for 16% of the time, Pallas kernels for 0%

commit v1 on v0

v1 whole, which is shorter than its diff:
```python
import functools

import jax
import jax.numpy as jnp
from jax import lax
from jax.experimental import pallas as pl
from jax.experimental.pallas import tpu as pltpu
from jax.sharding import PartitionSpec as P

highest = lax.Precision.HIGHEST
f32 = jnp.float32
bf16 = jnp.bfloat16
MESH = pl.DeviceIdType.MESH
NN = (((1,), (0,)), ((), ()))
NT = (((1,), (1,)), ((), ()))
TN = (((0,), (0,)), ((), ()))


def dot(a, b, dims=NN, precision=None):
    return lax.dot_general(a, b, dims, precision=precision, preferred_element_type=f32)


def two(x):
    high = x.astype(bf16)
    return high, (x - high.astype(f32)).astype(bf16)


def three(x):
    high = x.astype(bf16)
    rest = x - high.astype(f32)
    mid = rest.astype(bf16)
    return high, mid, (rest - mid.astype(f32)).astype(bf16)


def dot3(a, b, dims=NN):
    (ah, al), (bh, bl) = a, b
    return dot(ah, bh, dims) + (dot(ah, bl, dims) + dot(al, bh, dims))


def pick3(parts, onehot):
    high, mid, low = parts
    return (dot(low, onehot) + dot(mid, onehot)) + dot(high, onehot)


def iota(shape, axis):
    return lax.broadcasted_iota(jnp.int32, shape, axis)


def cholesky_block(aug, linv, b, width):
    n = aug.shape[0]
    lo = b * width
    d = aug[lo : lo + width, lo : lo + width]
    v = jnp.where(iota((width, width), 0) == iota((width, width), 1), 1.0, 0.0).astype(f32)
    below = iota((width, 1), 0)
    lane = iota((1, width), 1)
    diag = jnp.ones((width, 1), f32)
    for i in range(width):
        pivot = d[i : i + 1, i : i + 1]
        diag = jnp.where(below == i, pivot, diag)
        if i < width - 1:
            m = jnp.where(below > i, d[:, i : i + 1] * (1.0 / pivot), 0.0)
            d = d - m * d[i : i + 1, :]
            v = v - m * v[i : i + 1, :]
    v = v * lax.rsqrt(diag)
    rows = dot(v, aug[lo : lo + width, :], precision=highest)
    linv[lo : lo + width, :] = rows[:, n:]
    if lo + width < n:
        down = dot(rows[:, :n], rows, TN, highest)
        aug[lo + width :, :] = aug[lo + width :, :] - down[lo + width :, :]


def kernel(
    nrow, ncol, chunks, width,
    x, piv_row, piv_col, partner,
    perm_hbm, w_out, summed, upper_out, solved_out,
    onehot, picked, moved_in, from_left, from_right, to_right, to_left,
    panel, perm, product, core_in, reduce_in, totals, gram, gram_in, gram_parts, aug, linv,
    zr_s, zr_r, zl_s, zl_r, g1, g2_s, g2_r, g3, c_s, c_r, r_s, r_r, a_s, a_r, f_s, f_r, out_sem,
):
    rows, columns = x.shape
    n = panel.shape[1]
    tiles = columns // n
    chips = nrow // 2
    share = columns // nrow
    me = lax.axis_index("row")
    z = lax.axis_index("col")
    core = lax.rem(me, 2)
    chip = me // 2
    mate = me + 1 - 2 * core

    def remote(src, dst, ss, rs, dev):
        return pltpu.make_async_remote_copy(
            src_ref=src, dst_ref=dst, send_sem=ss, recv_sem=rs, device_id=dev, device_id_type=MESH
        )

    def peer(d):
        return lax.rem(chip + d, chips) * 2 + core

    def origin(d):
        return lax.rem(chip + chips - d, chips)

    barrier = pltpu.get_barrier_semaphore()

    @pl.when(z > 0)
    def _():
        pl.semaphore_signal(barrier, inc=1, device_id={"col": z - 1}, device_id_type=MESH)

    @pl.when(z < ncol - 1)
    def _():
        pl.semaphore_signal(barrier, inc=1, device_id={"col": z + 1}, device_id_type=MESH)

    pl.semaphore_signal(barrier, inc=1, device_id={"row": mate}, device_id_type=MESH)
    for d in range(1, chips):
        pl.semaphore_signal(barrier, inc=1, device_id={"row": peer(d)}, device_id_type=MESH)

    offset = z * columns
    local = piv_row[...] - offset
    mine = (local >= 0) & (local < columns)
    before = local < 0

    @pl.loop(0, tiles)
    def _(t):
        at = pl.multiple_of(t * n, n)
        onehot[pl.ds(at, n), :] = jnp.where(iota((n, n), 0) + at == local, 1.0, 0.0).astype(bf16)

    former_hot = jnp.where(iota((n, n), 0) == partner[...], 1.0, 0.0).astype(bf16)
    size = rows // chunks

    @pl.loop(0, chunks)
    def _(c):
        at = pl.ds(pl.multiple_of(c * size, size), size)
        picked[at, :] = pick3(three(x[at, :]), onehot[...])

    @pl.when(z == 0)
    def _():
        @pl.loop(0, chunks)
        def _(c):
            at = pl.ds(pl.multiple_of(c * size, size), size)
            moved_in[at, :] = pick3(three(x[at, :n]), former_hot)

    pl.semaphore_wait(
        barrier, chips + jnp.where(z > 0, 1, 0) + jnp.where(z < ncol - 1, 1, 0)
    )

    def right(c):
        at = pl.ds(pl.multiple_of(c * size, size), size)
        return remote(to_right.at[at, :], from_left.at[at, :], zr_s.at[c], zr_r.at[c], {"col": z + 1})

    def left(c):
        at = pl.ds(pl.multiple_of(c * size, size), size)
        return remote(to_left.at[at, :], from_right.at[at, :], zl_s.at[c], zl_r.at[c], {"col": z - 1})

    @pl.loop(0, chunks + ncol - 1)
    def _(t):
        c = t - z

        @pl.when((c >= 0) & (c < chunks))
        def _():
            at = pl.ds(pl.multiple_of(c * size, size), size)

            @pl.when(z > 0)
            def _():
                right(c).wait_recv()
                moved_in[at, :] = from_left[at, :]

            @pl.when(z < ncol - 1)
            def _():
                to_right[at, :] = jnp.where(mine, picked[at, :], moved_in[at, :])
                right(c).start()

        e = t - (ncol - 1 - z)

        @pl.when((e >= 0) & (e < chunks))
        def _():
            at = pl.ds(pl.multiple_of(e * size, size), size)

            @pl.when(z < ncol - 1)
            def _():
                left(e).wait_recv()
                panel[at, :] = jnp.where(mine, picked[at, :], from_right[at, :])

            @pl.when(z == ncol - 1)
            def _():
                panel[at, :] = picked[at, :]

            @pl.when(z > 0)
            def _():
                to_left[at, :] = panel[at, :]
                left(e).start()

    panel[...] = jnp.where(before, moved_in[...], panel[...])

    half = n // 2
    columns_of = panel[...].T
    gram[...] = dot(columns_of, panel[...], precision=highest)
    first = remote(gram, gram_in, g1.at[0], g1.at[1], {"row": mate})
    first.start()

    left_parts = two(columns_of)
    former = three(moved_in[...])
    wanted = piv_col[...] - offset
    usable = piv_col[...] >= n

    def out_copy(t):
        at = pl.ds(pl.multiple_of(t * n, n), n)
        return pltpu.make_async_copy(perm.at[:, at], perm_hbm.at[:, at], out_sem.at[t])

    @pl.loop(0, tiles)
    def _(t):
        at = pl.multiple_of(t * n, n)
        place = (iota((n, n), 1) + at == wanted) & usable
        place = jnp.where(place, 1.0, 0.0)
        keep = 1.0 - jnp.sum(place, axis=0, keepdims=True)
        tile = x[:, pl.ds(at, n)] * keep + pick3(former, place.astype(bf16))
        tile = jnp.where((z == 0) & (t == 0), panel[...], tile)
        perm[:, pl.ds(at, n)] = tile
        out_copy(t).start()
        product[pl.ds(at, n), :] = dot3(left_parts, two(tile)).T

    def part(owner):
        return pl.ds(pl.multiple_of(owner * share, share), share)

    def to_mate(c):
        return remote(product.at[part(2 * c + 1 - core), :], core_in.at[c], c_s.at[c], c_r.at[c], {"row": mate})

    for c in range(chips):
        to_mate(c).start()

    first.wait()
    mine_rows = pl.ds(pl.multiple_of(core * half, half), half)
    other_rows = pl.ds(pl.multiple_of((1 - core) * half, half), half)
    gram_parts[0, :, :] = gram[mine_rows, :] + gram_in[mine_rows, :]

    def gram_to(d):
        return remote(gram_parts.at[0], gram_parts.at[d], g2_s.at[d], g2_r.at[d], {"row": peer(d)})

    for d in range(1, chips):
        gram_to(d).start()

    for c in range(chips):
        to_mate(c).wait()
        totals[c, :, :] = product[part(2 * c + core), :] + core_in[c, :, :]

    def reduce_to(d):
        return remote(totals.at[lax.rem(chip + d, chips)], reduce_in.at[d], r_s.at[d], r_r.at[d], {"row": peer(d)})

    for d in range(1, chips):
        reduce_to(d).start()

    for d in range(1, chips):
        gram_to(d).wait()
    gram_half = jnp.zeros((half, n), f32)
    for d in range(chips):
        gram_half = gram_half + gram_parts[lax.rem(chip + chips - d, chips), :, :]
    aug[mine_rows, :n] = gram_half
    last = remote(aug.at[mine_rows, :n], aug.at[mine_rows, :n], g3.at[0], g3.at[1], {"row": mate})
    last.start()
    aug[:, n:] = jnp.where(iota((n, n), 0) == iota((n, n), 1), 1.0, 0.0).astype(f32)
    last.wait_send()
    remote(aug.at[other_rows, :n], aug.at[other_rows, :n], g3.at[0], g3.at[1], {"row": mate}).wait_recv()

    def gather_to(d):
        return remote(summed.at[part(me), :], summed.at[part(me), :], a_s.at[d], a_r.at[d], {"row": peer(d)})

    def gathered(d):
        at = part(origin(d) * 2 + core)
        return remote(summed.at[at, :], summed.at[at, :], a_s.at[d], a_r.at[d], {"row": peer(d)})

    def forward(d):
        at = part(origin(d) * 2 + core)
        return remote(summed.at[at, :], summed.at[at, :], f_s.at[d], f_r.at[d], {"row": mate})

    def forwarded(d):
        at = part(origin(d) * 2 + 1 - core)
        return remote(summed.at[at, :], summed.at[at, :], f_s.at[d], f_r.at[d], {"row": mate})

    def finish_reduce():
        total = totals[chip, :, :]
        for d in range(1, chips):
            reduce_to(d).wait()
            total = total + reduce_in[d, :, :]
        summed[part(me), :] = total
        for d in range(1, chips):
            gather_to(d).start()
        forward(0).start()

    def finish_gather():
        for d in range(1, chips):
            gathered(d).wait_recv()
            forward(d).start()

    blocks = n // width
    for b in range(blocks):
        cholesky_block(aug, linv, b, width)
        if b == blocks // 2 - 1:
            finish_reduce()
    finish_gather()

    inverse = dot(linv[...], linv[...], TN, highest)
    w_out[...] = dot(panel[...], inverse, precision=highest)
    own = summed[part(me), :]
    upper_out[...] = dot(linv[...], own, NT, highest)
    solved_out[...] = dot(inverse, own, NT, highest)

    for d in range(chips):
        forwarded(d).wait_recv()
    for d in range(1, chips):
        gather_to(d).wait_send()
    for d in range(chips):
        forward(d).wait_send()

    @pl.loop(0, chunks)
    def _(c):
        @pl.when(z < ncol - 1)
        def _():
            right(c).wait_send()

        @pl.when(z > 0)
        def _():
            left(c).wait_send()

    @pl.loop(0, tiles)
    def _(t):
        out_copy(t).wait()


def project(perm, w, summed, out):
    out[...] = perm[...] - dot3(two(w[...]), two(summed[...]), NT)


def hot(condition):
    return jnp.where(condition, 1.0, 0.0).astype(f32)


def per_device(nrow, ncol, matrix, pivots, sketch):
    rows, columns = matrix.shape
    n = pivots.shape[0]
    pieces = sketch.shape[1]
    positions = jnp.arange(n, dtype=jnp.int32)
    absent = ~jnp.any(pivots[None, :] == positions[:, None], axis=1)
    place = jnp.sum((absent[None, :] & (positions[None, :] < positions[:, None])).astype(jnp.int32), axis=1)
    rank = jnp.sum(((pivots[None, :] >= n) & (pivots[None, :] < pivots[:, None])).astype(jnp.int32), axis=1)
    partner = jnp.sum(
        jnp.where(absent[None, :] & (place[None, :] == rank[:, None]), positions[None, :], 0), axis=1
    )

    start = (lax.axis_index("col") * nrow + lax.axis_index("row")) * pieces
    spots = start + jnp.arange(pieces, dtype=jnp.int32)
    both = jnp.concatenate([pivots, partner])
    picks = jnp.dot(sketch, hot(spots[:, None] == both[None, :]), precision=highest)
    fronts_former = lax.psum(picks, ("row", "col"))

    chunks = 10
    width = 32
    chips = nrow // 2
    share = columns // nrow
    vmem = pl.BlockSpec(memory_space=pltpu.VMEM)
    full = pltpu.VMEM((rows, n), f32)
    dma = pltpu.SemaphoreType.DMA
    perm, w, summed, upper, solved = pl.pallas_call(
        functools.partial(kernel, nrow, ncol, chunks, width),
        out_shape=[
            jax.ShapeDtypeStruct((rows, columns), f32),
            jax.ShapeDtypeStruct((rows, n), f32),
            jax.ShapeDtypeStruct((columns, n), f32),
            jax.ShapeDtypeStruct((n, share), f32),
            jax.ShapeDtypeStruct((n, share), f32),
        ],
        in_specs=[vmem] * 4,
        out_specs=[pl.BlockSpec(memory_space=pl.ANY)] + [vmem] * 4,
        scratch_shapes=[
            pltpu.VMEM((columns, n), bf16),
            full, full, full, full, full, full, full,
            pltpu.VMEM((rows, columns), f32),
            pltpu.VMEM((columns, n), f32),
            pltpu.VMEM((chips, share, n), f32),
            pltpu.VMEM((chips, share, n), f32),
            pltpu.VMEM((chips, share, n), f32),
            pltpu.VMEM((n, n), f32),
            pltpu.VMEM((n, n), f32),
            pltpu.VMEM((chips, n // 2, n), f32),
            pltpu.VMEM((n, 2 * n), f32),
            pltpu.VMEM((n, n), f32),
            dma((chunks,)), dma((chunks,)), dma((chunks,)), dma((chunks,)),
            dma((2,)), dma((chips,)), dma((chips,)), dma((2,)),
            dma((chips,)), dma((chips,)), dma((chips,)), dma((chips,)),
            dma((chips,)), dma((chips,)), dma((chips,)), dma((chips,)),
            dma((columns // n,)),
        ],
        compiler_params=pltpu.CompilerParams(
            collective_id=0, has_side_effects=True, vmem_limit_bytes=56 * 1024 * 1024
        ),
        cost_estimate=pl.CostEstimate(
            flops=20 * rows * n * columns, bytes_accessed=8 * rows * columns, transcendentals=0
        ),
    )(matrix, pivots[None, :], pivots[:, None], partner[None, :])

    tile = 2 * n
    trailing = pl.pallas_call(
        project,
        grid=(columns // tile,),
        out_shape=jax.ShapeDtypeStruct((rows, columns), f32),
        in_specs=[
            pl.BlockSpec((rows, tile), lambda i: (0, i)),
            pl.BlockSpec((rows, n), lambda i: (0, 0)),
            pl.BlockSpec((tile, n), lambda i: (i, 0)),
        ],
        out_specs=pl.BlockSpec((rows, tile), lambda i: (0, i)),
        compiler_params=pltpu.CompilerParams(vmem_limit_bytes=56 * 1024 * 1024),
    )(perm, w, summed)

    into = (spots[None, :] == pivots[:, None]) & (pivots[:, None] >= n)
    leading = spots[None, :] == positions[:, None]
    gone = jnp.any(into | leading, axis=0)
    moved = jnp.where(gone[None, :], 0.0, sketch) + jnp.dot(
        fronts_former, hot(jnp.concatenate([leading, into])), precision=highest
    )
    new_sketch = moved - jnp.dot(fronts_former[:, :n], solved, precision=highest)
    return (upper, trailing, new_sketch)


def solution(mesh):
    return jax.shard_map(
        functools.partial(per_device, mesh.shape["row"], mesh.shape["col"]),
        mesh=mesh,
        in_specs=(P("row", "col"), P(), P(None, ("col", "row"))),
        out_specs=(P(None, ("col", "row")), P("row", "col"), P(None, ("col", "row"))),
        check_vma=False,
    )
```

time: 375 us -> 161 us (0.43)
  waiting for transfers between devices: 203 us -> 21.8 us
  Pallas kernels: 0 us -> 112 us
  other arithmetic: 79.1 us -> 3.53 us
  local copies, waits for them, and re-layouts: 46.5 us -> 2.2 us
  matrix products: 29.8 us -> 6.28 us
    psum x3 -> x1, waiting for transfers between devices: 203 us -> 21.8 us  [per_device(): fronts_former = lax.psum(picks, ('row', 'col'))]
    pallas_call x0 -> x2, Pallas kernels: none -> 112 us  [the longest x1 104 us: per_device(): pl.pallas_call(functools.partial(kernel, nrow, ncol, chunks, width), out_...]
    another operation x11 -> x0, other arithmetic: 54.3 us -> none  [the longest x7 34.6 us: per_device(): lower_factor = jnp.linalg.cholesky(gram_total)]
    gather x10 -> x0, local copies, waits for them, and re-layouts: 27.7 us -> none  [the longest x4 17.6 us: arrange(): leading = jnp.take(fronts, jnp.clip(global_pos, 0, panel_cols - 1), axis=1)]
    dot_general x4 -> x3, matrix products: 21.1 us -> 6.28 us  [the longest x1 2.56 us: per_device(): jnp.dot(sketch, hot(spots[:, None] == both[None, :]), precision=highest)]
    scatter x2 -> x0, other arithmetic: 13.6 us -> none  [arrange(): source.at[:, target].set(jnp.take(former, anchor, axis=1), mode='drop')]
    another operation x11 -> x0, matrix products: 8.68 us -> none  [the longest x3 5.7 us: per_device(): lax.linalg.triangular_solve(lower_factor, summed, left_side=True, lower=T...]
    sort x2 -> x0, other arithmetic: 6.33 us -> none  [the longest x1 3.17 us: pairing(): vacated = jnp.sort(jnp.where(pivots >= panel_cols, pivots, sentinel_value))]
  transfers between devices with their start and end apart: 3 -> 1, of which waited for: 3 -> 1; matrix products, arithmetic and copies ran while one was open for 16% -> 1% of each run, Pallas kernels for 0% -> 70%
where the time goes in v1:
time: 161 us; the launch traced here: 160 us
  Pallas kernels  112 us (70%)
  waiting for transfers between devices  21.8 us (14%)
  between operations  14.1 us (9%)
  matrix products  6.28 us (4%)
  other arithmetic  3.53 us (2%)
  local copies, waits for them, and re-layouts  2.2 us (1%)
    pallas_call x1, Pallas kernels, per_device(): pl.pallas_call(functools.partial(kernel, nrow, ncol, chunks, width), out_...  104 us
    psum x1, waiting for transfers between devices, per_device(): fronts_former = lax.psum(picks, ('row', 'col'))  21.8 us
    pallas_call x1, Pallas kernels, per_device(): pl.pallas_call(project, grid=(columns // tile,), out_shape=jax.ShapeDtype...  7.77 us
  transfers between devices with their start and end apart: 1, of which 1 were waited for; matrix products, arithmetic and copies ran while one was open for 1% of the time, Pallas kernels for 70%

profile of v1, /device:TPU:0, one launch (start us, length us, event | category | flops | bytes accessed | tf_op | source)
XLA Modules:
  0.0 160.1 jit_solution(8063993911864464450)
XLA Ops:
  7.2 0.0 all-reduce.2.cloned.1.call-start
  7.2 0.7 broadcast_compare_fusion
  7.9 1.0 or_reduce_fusion
  8.9 1.0 convert_reduce_fusion
  9.9 0.2 select_reduce_fusion
  10.1 0.0 copy-start.3
  10.1 0.7 pad_add_fusion
  10.8 2.6 %convolution_bitcast_fusion = f32[264,512]{1,0:T(8,128)} fusion(f32[264,256]{1,0:T(8,128)} %param.5, s32[512]{0:T(512)S(1)} %pad_add_fusion, s32[256]{0:T(256)S(1)} %iota_add_fusion), kind=kOutput, calls=%fused_computation | convolution fusion | flops 415498240 | bytes 814080 | tf_op jit(solution)/shard_map/dot_general | solution.py:350
  13.3 0.0 all-reduce.2.cloned.1.call-update
  13.3 1.5 copy.7.piv_col
  14.8 0.0 copy-done.3
  14.8 104.3 %shard_map.58 = (f32[640,2048]{1,0:T(8,128)}, f32[640,256]{1,0:T(8,128)}, f32[2048,256]{1,0:T(8,128)}, f32[256,256]{1,0:T(8,128)}, f32[256,256]{1,0:T(8,128)}) custom-call(f32[640,2048]{1,0:T(8,128)} %x.1, s32[1,256]{1,0:T(1,128)} %bitcast.9, s32[256,1]{1,0:T(8,128)} %copy.7.piv_col, s32[1,256]{1,0:T(1,128)} %bitcast.10), custom_call_target="tpu_custom_call" | custom-call | flops 6710886400 | bytes 10485760 | tf_op jit(solution)/shard_map/pallas_call | solution.py:360
  119.1 0.0 copy-start
  119.2 0.0 copy-start.2
  119.2 0.0 copy-start.1
  119.2 7.8 %shard_map.59 = f32[640,2048]{1,0:T(8,128)} custom-call(f32[640,2048]{1,0:T(8,128)} %get-tuple-element.9.perm, f32[640,256]{1,0:T(8,128)} %get-tuple-element.10.w, f32[2048,256]{1,0:T(8,128)} %get-tuple-element.11.summed), custom_call_target="tpu_custom_call" | custom-call | tf_op jit(solution)/shard_map/pallas_call | solution.py:399
  126.9 21.8 %all-reduce.2.cloned.1.call-done = f32[264,512]{1,0:T(8,128)} async-done(((f32[264,512]{1,0:T(8,128)}), f32[264,512]{1,0:T(8,128)}) %all-reduce.2.cloned.1.call-update) | async-done | bytes 540688 | tf_op jit(solution)/shard_map/psum | solution.py:351
  148.8 0.0 copy-done
  148.8 1.7 %convolution_add_fusion = f32[264,256]{1,0:T(8,128)S(1)} fusion(f32[264,512]{1,0:T(8,128)} %all-reduce.2.cloned.1.call-done, pred[256,256]{1,0:T(32,128)(4,1)S(1)} %get-tuple-element.15, pred[256,256]{1,0:T(32,128)(4,1)S(1)} %get-tuple-element.16, f32[264,256]{1,0:T(8,128)S(1)} %copy-done, pred[256]{0:T(512)(128)(4,1)S(1)} %get-tuple-element.13), kind=kOutput, calls=%fused_computation.2 | convolution fusion | flops 415633408 | bytes 1212672 | tf_op jit(solution)/shard_map/dot_general | solution.py:415
  150.5 0.0 copy-done.2
  150.5 2.1 %convolution_subtract_fusion = f32[264,256]{1,0:T(8,128)} fusion(f32[264,256]{1,0:T(8,128)S(1)} %convolution_add_fusion, f32[256,256]{1,0:T(8,128)S(1)} %copy-done.2, f32[264,512]{1,0:T(8,128)} %all-reduce.2.cloned.1.call-done), kind=kOutput, calls=%fused_computation.1 | convolution fusion | flops 207685632 | bytes 1073152 | tf_op jit(solution)/shard_map/dot_general | solution.py:418
  152.5 0.0 copy-done.1
  152.5 0.7 copy.14
  (2 shorter events, 0.0 us)
Async XLA Ops:
  7.2 141.6 %all-reduce.2.cloned.1.call-start = ((), (), s32[]{:S(2)}) async-start(), calls=%async_computation | async-start | bytes 1081344 | tf_op jit(solution)/shard_map/psum | solution.py:351
  10.1 4.8 %copy-start.3 = (s32[256]{0:T(256)}, s32[256]{0:T(256)S(1)}, u32[]{:S(2)}) copy-start(s32[256]{0:T(256)S(1)} %select_reduce_fusion) | copy-start | bytes 3076
  119.1 29.6 %copy-start = (f32[264,256]{1,0:T(8,128)S(1)}, f32[264,256]{1,0:T(8,128)}, u32[]{:S(2)}) copy-start(f32[264,256]{1,0:T(8,128)} %param.5) | copy-start | bytes 811012
  119.2 31.3 %copy-start.2 = (f32[256,256]{1,0:T(8,128)S(1)}, f32[256,256]{1,0:T(8,128)}, u32[]{:S(2)}) copy-start(f32[256,256]{1,0:T(8,128)} %get-tuple-element.12) | copy-start | bytes 786436
  119.2 33.4 %copy-start.1 = (f32[256,256]{1,0:T(8,128)S(1)}, f32[256,256]{1,0:T(8,128)}, u32[]{:S(2)}) copy-start(f32[256,256]{1,0:T(8,128)} %get-tuple-element.22) | copy-start | bytes 786436
Sparse Core Ops, SparseCore 0:
  13.5 135.2 all-reduce.1

commit v2 on v1

--- a/solution.py
+++ b/solution.py
@@ -49,33 +49,36 @@
 def cholesky_block(aug, linv, b, width):
     n = aug.shape[0]
     lo = b * width
-    d = aug[lo : lo + width, lo : lo + width]
-    v = jnp.where(iota((width, width), 0) == iota((width, width), 1), 1.0, 0.0).astype(f32)
-    below = iota((width, 1), 0)
-    lane = iota((1, width), 1)
-    diag = jnp.ones((width, 1), f32)
+    eye = jnp.where(iota((width, width), 0) == iota((width, width), 1), 1.0, 0.0).astype(f32)
+    both = jnp.concatenate([aug[lo : lo + width, lo : lo + width], eye], axis=1)
+    below = iota((width, 2 * width), 0)
+    diag = jnp.ones((width, 2 * width), f32)
     for i in range(width):
-        pivot = d[i : i + 1, i : i + 1]
+        across = jnp.broadcast_to(both[:, i : i + 1], both.shape)
+        pivot = across[i : i + 1, :]
         diag = jnp.where(below == i, pivot, diag)
         if i < width - 1:
-            m = jnp.where(below > i, d[:, i : i + 1] * (1.0 / pivot), 0.0)
-            d = d - m * d[i : i + 1, :]
-            v = v - m * v[i : i + 1, :]
-    v = v * lax.rsqrt(diag)
-    rows = dot(v, aug[lo : lo + width, :], precision=highest)
+            scaled = both[i : i + 1, :] * (1.0 / pivot)
+            both = both - jnp.where(below > i, across, 0.0) * scaled
+    inverse = both[:, width:] * lax.rsqrt(diag[:, :width])
+    rows = dot3(two(inverse), two(aug[lo : lo + width, :]))
     linv[lo : lo + width, :] = rows[:, n:]
     if lo + width < n:
-        down = dot(rows[:, :n], rows, TN, highest)
-        aug[lo + width :, :] = aug[lo + width :, :] - down[lo + width :, :]
+        start = (lo + width) // 128 * 128
+        high, low = two(rows)
+        left = (high[:, start:n], low[:, start:n])
+        aug[start:, start:] = aug[start:, start:] - dot3(left, (high[:, start:], low[:, start:]), TN)
 
 
 def kernel(
     nrow, ncol, chunks, width,
-    x, piv_row, piv_col, partner,
-    perm_hbm, w_out, summed, upper_out, solved_out,
+    x, pivots, sketch,
+    perm_hbm, w_high, w_low, s_high, s_low, upper_out, sketch_out,
     onehot, picked, moved_in, from_left, from_right, to_right, to_left,
-    panel, perm, product, core_in, reduce_in, totals, gram, gram_in, gram_parts, aug, linv,
+    panel, perm, product, summed, core_in, reduce_in, totals, gram, gram_in, gram_parts, aug, linv,
+    sk_pad, sk_pick, sk_in, sk_part, sk_all,
     zr_s, zr_r, zl_s, zl_r, g1, g2_s, g2_r, g3, c_s, c_r, r_s, r_r, a_s, a_r, f_s, f_r, out_sem,
+    ks_s, ks_r, kz_s, kz_r, ka_s, ka_r, kf_s, kf_r,
 ):
     rows, columns = x.shape
     n = panel.shape[1]
@@ -99,22 +102,59 @@
     def origin(d):
         return lax.rem(chip + chips - d, chips)
 
+    def beside(d):
+        return {"row": lax.rem(me + d, nrow)}
+
+    def along(d):
+        return {"col": lax.rem(z + d, ncol)}
+
     barrier = pltpu.get_barrier_semaphore()
 
-    @pl.when(z > 0)
-    def _():
-        pl.semaphore_signal(barrier, inc=1, device_id={"col": z - 1}, device_id_type=MESH)
-
-    @pl.when(z < ncol - 1)
-    def _():
-        pl.semaphore_signal(barrier, inc=1, device_id={"col": z + 1}, device_id_type=MESH)
-
-    pl.semaphore_signal(barrier, inc=1, device_id={"row": mate}, device_id_type=MESH)
-    for d in range(1, chips):
-        pl.semaphore_signal(barrier, inc=1, device_id={"row": peer(d)}, device_id_type=MESH)
+    @pl.loop(1, nrow)
+    def _(d):
+        pl.semaphore_signal(barrier, inc=1, device_id=beside(d), device_id_type=MESH)
+
+    @pl.loop(1, ncol)
+    def _(d):
+        pl.semaphore_signal(barrier, inc=1, device_id=along(d), device_id_type=MESH)
+
+    def turned(row):
+        return jnp.sum(jnp.where(iota((n, n), 0) == iota((n, n), 1), row, 0.0), axis=1, keepdims=True)
+
+    row = pivots[...].astype(f32)
+    col = turned(row)
+    pos_row = iota((1, n), 1).astype(f32)
+    pos_col = iota((n, 1), 0).astype(f32)
+    absent_row = 1.0 - jnp.sum(jnp.where(col == pos_row, 1.0, 0.0), axis=0, keepdims=True)
+    absent_col = 1.0 - jnp.sum(jnp.where(row == pos_col, 1.0, 0.0), axis=1, keepdims=True)
+    rank_col = jnp.sum(jnp.where(pos_row < pos_col, absent_row, 0.0), axis=1, keepdims=True)
+    rank_row = jnp.sum(jnp.where((col >= n) & (col < row), 1.0, 0.0), axis=0, keepdims=True)
+    taken = jnp.where(rank_col == rank_row, absent_col * pos_col, 0.0)
+    partner = jnp.sum(taken, axis=0, keepdims=True)
+    piv_col = col.astype(jnp.int32)
+    both_col = jnp.concatenate([piv_col, turned(partner).astype(jnp.int32)], axis=0)
+    partner = partner.astype(jnp.int32)
+
+    sk, pieces = sketch.shape
+    slots = sk_pick.shape[0] // nrow
+    spots = iota((1, pieces), 1) + (z * nrow + me) * pieces
+    sk_pad[...] = jnp.zeros_like(sk_pad)
+    sk_pad[:sk, :] = sketch[...]
+    sk_hot = jnp.where(both_col == spots, 1.0, 0.0).astype(bf16)
+    k_high, k_mid, k_low = three(sk_pad[...])
+    sk_pick[...] = (dot(sk_hot, k_low, NT) + dot(sk_hot, k_mid, NT)) + dot(sk_hot, k_high, NT)
+
+    def slots_of(owner):
+        return pl.ds(pl.multiple_of(owner * slots, slots), slots)
+
+    def sk_reduce(d):
+        return remote(sk_pick.at[slots_of(lax.rem(me + d, nrow)), :], sk_in.at[d], ks_s.at[d], ks_r.at[d], beside(d))
+
+    def sk_along(d):
+        return remote(sk_part.at[0], sk_part.at[d], kz_s.at[d], kz_r.at[d], along(d))
 
     offset = z * columns
-    local = piv_row[...] - offset
+    local = pivots[...] - offset
     mine = (local >= 0) & (local < columns)
     before = local < 0
 
@@ -123,7 +163,13 @@
         at = pl.multiple_of(t * n, n)
         onehot[pl.ds(at, n), :] = jnp.where(iota((n, n), 0) + at == local, 1.0, 0.0).astype(bf16)
 
-    former_hot = jnp.where(iota((n, n), 0) == partner[...], 1.0, 0.0).astype(bf16)
+    pl.semaphore_wait(barrier, nrow + ncol - 2)
+
+    @pl.loop(1, nrow)
+    def _(d):
+        sk_reduce(d).start()
+
+    former_hot = jnp.where(iota((n, n), 0) == partner, 1.0, 0.0).astype(bf16)
     size = rows // chunks
 
     @pl.loop(0, chunks)
@@ -138,10 +184,6 @@
             at = pl.ds(pl.multiple_of(c * size, size), size)
             moved_in[at, :] = pick3(three(x[at, :n]), former_hot)
 
-    pl.semaphore_wait(
-        barrier, chips + jnp.where(z > 0, 1, 0) + jnp.where(z < ncol - 1, 1, 0)
-    )
-
     def right(c):
         at = pl.ds(pl.multiple_of(c * size, size), size)
         return remote(to_right.at[at, :], from_left.at[at, :], zr_s.at[c], zr_r.at[c], {"col": z + 1})
@@ -198,8 +240,19 @@
 
     left_parts = two(columns_of)
     former = three(moved_in[...])
-    wanted = piv_col[...] - offset
-    usable = piv_col[...] >= n
+    wanted = piv_col - offset
+    usable = piv_col >= n
+
+    first.wait()
+    mine_rows = pl.ds(pl.multiple_of(core * half, half), half)
+    other_rows = pl.ds(pl.multiple_of((1 - core) * half, half), half)
+    gram_parts[0, :, :] = gram[mine_rows, :] + gram_in[mine_rows, :]
+
+    def gram_to(d):
+        return remote(gram_parts.at[0], gram_parts.at[d], g2_s.at[d], g2_r.at[d], {"row": peer(d)})
+
+    for d in range(1, chips):
+        gram_to(d).start()
 
     def out_copy(t):
         at = pl.ds(pl.multiple_of(t * n, n), n)
@@ -226,17 +279,6 @@
     for c in range(chips):
         to_mate(c).start()
 
-    first.wait()
-    mine_rows = pl.ds(pl.multiple_of(core * half, half), half)
-    other_rows = pl.ds(pl.multiple_of((1 - core) * half, half), half)
-    gram_parts[0, :, :] = gram[mine_rows, :] + gram_in[mine_rows, :]
-
-    def gram_to(d):
-        return remote(gram_parts.at[0], gram_parts.at[d], g2_s.at[d], g2_r.at[d], {"row": peer(d)})
-
-    for d in range(1, chips):
-        gram_to(d).start()
-
     for c in range(chips):
         to_mate(c).wait()
         totals[c, :, :] = product[part(2 * c + core), :] + core_in[c, :, :]
@@ -246,6 +288,14 @@
 
     for d in range(1, chips):
         reduce_to(d).start()
+
+    @pl.loop(1, nrow)
+    def _(d):
+        sk_reduce(d).wait()
+
+    sk_part[0, :, :] = sk_pick[slots_of(me), :] + jnp.sum(sk_in[1:, :, :], axis=0)
+    for d in range(1, ncol):
+        sk_along(d).start()
 
     for d in range(1, chips):
         gram_to(d).wait()
@@ -274,6 +324,22 @@
         at = part(origin(d) * 2 + 1 - core)
         return remote(summed.at[at, :], summed.at[at, :], f_s.at[d], f_r.at[d], {"row": mate})
 
+    def sk_gather_to(d):
+        at = slots_of(me)
+        return remote(sk_all.at[at, :], sk_all.at[at, :], ka_s.at[d], ka_r.at[d], {"row": peer(d)})
+
+    def sk_gathered(d):
+        at = slots_of(origin(d) * 2 + core)
+        return remote(sk_all.at[at, :], sk_all.at[at, :], ka_s.at[d], ka_r.at[d], {"row": peer(d)})
+
+    def sk_forward(d):
+        at = slots_of(origin(d) * 2 + core)
+        return remote(sk_all.at[at, :], sk_all.at[at, :], kf_s.at[d], kf_r.at[d], {"row": mate})
+
+    def sk_forwarded(d):
+        at = slots_of(origin(d) * 2 + 1 - core)
+        return remote(sk_all.at[at, :], sk_all.at[at, :], kf_s.at[d], kf_r.at[d], {"row": mate})
+
     def finish_reduce():
         total = totals[chip, :, :]
         for d in range(1, chips):
@@ -283,6 +349,12 @@
         for d in range(1, chips):
             gather_to(d).start()
         forward(0).start()
+        for d in range(1, ncol):
+            sk_along(d).wait()
+        sk_all[slots_of(me), :] = jnp.sum(sk_part[...], axis=0)
+        for d in range(1, chips):
+            sk_gather_to(d).start()
+        sk_forward(0).start()
 
     def finish_gather():
         for d in range(1, chips):
@@ -295,19 +367,42 @@
         if b == blocks // 2 - 1:
             finish_reduce()
     finish_gather()
-
-    inverse = dot(linv[...], linv[...], TN, highest)
-    w_out[...] = dot(panel[...], inverse, precision=highest)
-    own = summed[part(me), :]
-    upper_out[...] = dot(linv[...], own, NT, highest)
-    solved_out[...] = dot(inverse, own, NT, highest)
+    for d in range(1, chips):
+        sk_gathered(d).wait_recv()
+        sk_forward(d).start()
+
+    inverse = dot3(two(linv[...]), two(linv[...]), TN)
+    w_high[...], w_low[...] = two(dot3(two(panel[...]), two(inverse)))
+    own = two(summed[part(me), :])
+    upper_out[...] = dot3(two(linv[...]), own, NT)
+    solved = dot3(two(inverse), own, NT)
 
     for d in range(chips):
         forwarded(d).wait_recv()
+
+    @pl.loop(0, tiles)
+    def _(t):
+        at = pl.ds(pl.multiple_of(t * n, n), n)
+        high, low = two(summed[at, :].T)
+        s_high[:, at] = high
+        s_low[:, at] = low
+
+    for d in range(chips):
+        sk_forwarded(d).wait_recv()
+    into = jnp.where((spots == piv_col) & (piv_col >= n), 1.0, 0.0)
+    leading = jnp.where(spots == iota((n, 1), 0), 1.0, 0.0)
+    chosen = jnp.concatenate([leading, into], axis=0)
+    stay = 1.0 - jnp.sum(chosen, axis=0, keepdims=True)
+    turned_all = sk_all[...].T
+    changed = pick3(three(turned_all), chosen.astype(bf16)) - dot3(two(turned_all[:, :n]), two(solved))
+    sketch_out[...] = sketch[...] * stay + changed[:sk, :]
+
     for d in range(1, chips):
         gather_to(d).wait_send()
+        sk_gather_to(d).wait_send()
     for d in range(chips):
         forward(d).wait_send()
+        sk_forward(d).wait_send()
 
     @pl.loop(0, chunks)
     def _(c):
@@ -324,54 +419,42 @@
         out_copy(t).wait()
 
 
-def project(perm, w, summed, out):
-    out[...] = perm[...] - dot3(two(w[...]), two(summed[...]), NT)
-
-
-def hot(condition):
-    return jnp.where(condition, 1.0, 0.0).astype(f32)
+def project(perm, w_high, w_low, s_high, s_low, out):
+    out[...] = perm[...] - dot3((w_high[...], w_low[...]), (s_high[...], s_low[...]))
 
 
 def per_device(nrow, ncol, matrix, pivots, sketch):
     rows, columns = matrix.shape
     n = pivots.shape[0]
-    pieces = sketch.shape[1]
-    positions = jnp.arange(n, dtype=jnp.int32)
-    absent = ~jnp.any(pivots[None, :] == positions[:, None], axis=1)
-    place = jnp.sum((absent[None, :] & (positions[None, :] < positions[:, None])).astype(jnp.int32), axis=1)
-    rank = jnp.sum(((pivots[None, :] >= n) & (pivots[None, :] < pivots[:, None])).astype(jnp.int32), axis=1)
-    partner = jnp.sum(
-        jnp.where(absent[None, :] & (place[None, :] == rank[:, None]), positions[None, :], 0), axis=1
-    )
-
-    start = (lax.axis_index("col") * nrow + lax.axis_index("row")) * pieces
-    spots = start + jnp.arange(pieces, dtype=jnp.int32)
-    both = jnp.concatenate([pivots, partner])
-    picks = jnp.dot(sketch, hot(spots[:, None] == both[None, :]), precision=highest)
-    fronts_former = lax.psum(picks, ("row", "col"))
-
+    sk, pieces = sketch.shape
+    padded = (sk + 127) // 128 * 128
     chunks = 10
-    width = 32
+    width = 64
     chips = nrow // 2
     share = columns // nrow
+    slots = 2 * n // nrow
     vmem = pl.BlockSpec(memory_space=pltpu.VMEM)
     full = pltpu.VMEM((rows, n), f32)
     dma = pltpu.SemaphoreType.DMA
-    perm, w, summed, upper, solved = pl.pallas_call(
+    shape = jax.ShapeDtypeStruct
+    perm, w_high, w_low, s_high, s_low, upper, new_sketch = pl.pallas_call(
         functools.partial(kernel, nrow, ncol, chunks, width),
         out_shape=[
-            jax.ShapeDtypeStruct((rows, columns), f32),
-            jax.ShapeDtypeStruct((rows, n), f32),
-            jax.ShapeDtypeStruct((columns, n), f32),
-            jax.ShapeDtypeStruct((n, share), f32),
-            jax.ShapeDtypeStruct((n, share), f32),
+            shape((rows, columns), f32),
+            shape((rows, n), bf16),
+            shape((rows, n), bf16),
+            shape((n, columns), bf16),
+            shape((n, columns), bf16),
+            shape((n, share), f32),
+            shape((sk, pieces), f32),
         ],
-        in_specs=[vmem] * 4,
-        out_specs=[pl.BlockSpec(memory_space=pl.ANY)] + [vmem] * 4,
+        in_specs=[vmem] * 3,
+        out_specs=[pl.BlockSpec(memory_space=pl.ANY)] + [vmem] * 6,
         scratch_shapes=[
             pltpu.VMEM((columns, n), bf16),
             full, full, full, full, full, full, full,
             pltpu.VMEM((rows, columns), f32),
+            pltpu.VMEM((columns, n), f32),
             pltpu.VMEM((columns, n), f32),
             pltpu.VMEM((chips, share, n), f32),
             pltpu.VMEM((chips, share, n), f32),
@@ -381,11 +464,18 @@
             pltpu.VMEM((chips, n // 2, n), f32),
             pltpu.VMEM((n, 2 * n), f32),
             pltpu.VMEM((n, n), f32),
+            pltpu.VMEM((padded, pieces), f32),
+            pltpu.VMEM((2 * n, padded), f32),
+            pltpu.VMEM((nrow, slots, padded), f32),
+            pltpu.VMEM((ncol, slots, padded), f32),
+            pltpu.VMEM((2 * n, padded), f32),
             dma((chunks,)), dma((chunks,)), dma((chunks,)), dma((chunks,)),
             dma((2,)), dma((chips,)), dma((chips,)), dma((2,)),
             dma((chips,)), dma((chips,)), dma((chips,)), dma((chips,)),
             dma((chips,)), dma((chips,)), dma((chips,)), dma((chips,)),
             dma((columns // n,)),
+            dma((nrow,)), dma((nrow,)), dma((ncol,)), dma((ncol,)),
+            dma((chips,)), dma((chips,)), dma((chips,)), dma((chips,)),
         ],
         compiler_params=pltpu.CompilerParams(
             collective_id=0, has_side_effects=True, vmem_limit_bytes=56 * 1024 * 1024
@@ -393,29 +483,19 @@
         cost_estimate=pl.CostEstimate(
             flops=20 * rows * n * columns, bytes_accessed=8 * rows * columns, transcendentals=0
         ),
-    )(matrix, pivots[None, :], pivots[:, None], partner[None, :])
+    )(matrix, pivots[None, :], sketch)
 
     tile = 2 * n
+    whole = pl.BlockSpec((rows, n), lambda i: (0, 0))
+    across = pl.BlockSpec((n, tile), lambda i: (0, i))
     trailing = pl.pallas_call(
         project,
         grid=(columns // tile,),
         out_shape=jax.ShapeDtypeStruct((rows, columns), f32),
-        in_specs=[
-            pl.BlockSpec((rows, tile), lambda i: (0, i)),
-            pl.BlockSpec((rows, n), lambda i: (0, 0)),
-            pl.BlockSpec((tile, n), lambda i: (i, 0)),
-        ],
+        in_specs=[pl.BlockSpec((rows, tile), lambda i: (0, i)), whole, whole, across, across],
         out_specs=pl.BlockSpec((rows, tile), lambda i: (0, i)),
         compiler_params=pltpu.CompilerParams(vmem_limit_bytes=56 * 1024 * 1024),
-    )(perm, w, summed)
-
-    into = (spots[None, :] == pivots[:, None]) & (pivots[:, None] >= n)
-    leading = spots[None, :] == positions[:, None]
-    gone = jnp.any(into | leading, axis=0)
-    moved = jnp.where(gone[None, :], 0.0, sketch) + jnp.dot(
-        fronts_former, hot(jnp.concatenate([leading, into])), precision=highest
-    )
-    new_sketch = moved - jnp.dot(fronts_former[:, :n], solved, precision=highest)
+    )(perm, w_high, w_low, s_high, s_low)
     return (upper, trailing, new_sketch)
 
 

time: 161 us -> 116 us (0.72)
  waiting for transfers between devices: 21.8 us -> 0 us
  between operations: 14.1 us -> 0.66 us
  matrix products: 6.28 us -> 0 us
  other arithmetic: 3.53 us -> 0 us
  Pallas kernels: 112 us -> 114 us
    psum x1 -> x0, waiting for transfers between devices: 21.8 us -> none  [per_device(): fronts_former = lax.psum(picks, ('row', 'col'))]
    dot_general x3 -> x0, matrix products: 6.28 us -> none  [the longest x1 2.56 us: per_device(): jnp.dot(sketch, hot(spots[:, None] == both[None, :]), precision=highest)]
    pallas_call x1, Pallas kernels: 104 us -> 106 us  [per_device(): pl.pallas_call(functools.partial(kernel, nrow, ncol, chunks, width), out_...]
  transfers between devices with their start and end apart: 1 -> 0, of which waited for: 1 -> 0; matrix products, arithmetic and copies ran while one was open for 1% -> 0% of each run, Pallas kernels for 70% -> 0%
where the time goes in v2:
time: 116 us
  Pallas kernels  114 us (98%)
  local copies, waits for them, and re-layouts  1.42 us (1%)
    pallas_call x1, Pallas kernels, per_device(): pl.pallas_call(functools.partial(kernel, nrow, ncol, chunks, width), out_...  106 us
    pallas_call x1, Pallas kernels, per_device(): pl.pallas_call(project, grid=(columns // tile,), out_shape=jax.ShapeDtype...  7.32 us

profile of v2, /device:TPU:0, one launch (start us, length us, event | category | flops | bytes accessed | tf_op | source)
XLA Modules:
  0.0 115.7 jit_solution(16057167838036958613)
XLA Ops:
  0.6 106.3 %shard_map.58 = (f32[640,2048]{1,0:T(8,128)}, bf16[640,256]{1,0:T(8,128)(2,1)}, bf16[640,256]{1,0:T(8,128)(2,1)}, bf16[256,2048]{1,0:T(8,128)(2,1)}, bf16[256,20...) custom-call(f32[640,2048]{1,0:T(8,128)} %x.1, s32[1,256]{1,0:T(1,128)} %bitcast.1, f32[264,256]{1,0:T(8,128)} %sketch.1), custom_call_target="tpu_custom_call" | custom-call | flops 6710886400 | bytes 10485760 | tf_op jit(solution)/shard_map/pallas_call | solution.py:440
  107.0 0.0 copy-start.1
  107.0 0.0 copy-start
  107.0 7.3 %shard_map.59 = f32[640,2048]{1,0:T(8,128)} custom-call(f32[640,2048]{1,0:T(8,128)} %get-tuple-element.11.perm, bf16[640,256]{1,0:T(8,128)(2,1)} %get-tuple-element.12.w_high, bf16[640,256]{1,0:T(8,128)(2,1)} %get-tuple-element.13.w_low, bf16[256,2048]{1,0:T(8,128)(2,1)} %get-tuple-element.14.s_high, bf16[256,2048]{1,0:T(8,128)(2,1)} %get-tuple-element.15.s_low), custom_call_target="tpu_custom_call" | custom-call | tf_op jit(solution)/shard_map/pallas_call | solution.py:491
  114.3 0.0 copy-done.1
  114.3 0.7 copy.8
  115.0 0.0 copy-done
  115.0 0.7 copy.9
Async XLA Ops:
  107.0 7.3 %copy-start.1 = (f32[256,256]{1,0:T(8,128)S(1)}, f32[256,256]{1,0:T(8,128)}, u32[]{:S(2)}) copy-start(f32[256,256]{1,0:T(8,128)} %get-tuple-element.20) | copy-start | bytes 786436
  107.0 8.0 %copy-start = (f32[264,256]{1,0:T(8,128)S(1)}, f32[264,256]{1,0:T(8,128)}, u32[]{:S(2)}) copy-start(f32[264,256]{1,0:T(8,128)} %get-tuple-element.22) | copy-start | bytes 811012

commit v3 on v2

--- a/solution.py
+++ b/solution.py
@@ -34,12 +34,17 @@
 
 def dot3(a, b, dims=NN):
     (ah, al), (bh, bl) = a, b
+    ((i,), (j,)), _ = dims
+    if ah.shape[i] % 64 == 0:
+        left = jnp.concatenate([al, ah, ah], axis=i)
+        return dot(left, jnp.concatenate([bh, bl, bh], axis=j), dims)
     return dot(ah, bh, dims) + (dot(ah, bl, dims) + dot(al, bh, dims))
 
 
 def pick3(parts, onehot):
     high, mid, low = parts
-    return (dot(low, onehot) + dot(mid, onehot)) + dot(high, onehot)
+    left = jnp.concatenate([low, mid, high], axis=1)
+    return dot(left, jnp.concatenate([onehot] * 3, axis=0))
 
 
 def iota(shape, axis):
@@ -53,14 +58,21 @@
     both = jnp.concatenate([aug[lo : lo + width, lo : lo + width], eye], axis=1)
     below = iota((width, 2 * width), 0)
     diag = jnp.ones((width, 2 * width), f32)
-    for i in range(width):
-        across = jnp.broadcast_to(both[:, i : i + 1], both.shape)
-        pivot = across[i : i + 1, :]
-        diag = jnp.where(below == i, pivot, diag)
-        if i < width - 1:
-            scaled = both[i : i + 1, :] * (1.0 / pivot)
-            both = both - jnp.where(below > i, across, 0.0) * scaled
-    inverse = both[:, width:] * lax.rsqrt(diag[:, :width])
+    group = 4
+    for first in range(0, width, group):
+        across = [
+            jnp.broadcast_to(both[:, i : i + 1], both.shape) for i in range(first, first + group)
+        ]
+        for k in range(group):
+            i = first + k
+            inv = 1.0 / across[k][i : i + 1, :]
+            diag = jnp.where(below == i, inv, diag)
+            scaled = both[i : i + 1, :] * inv
+            column = jnp.where(below > i, across[k], 0.0)
+            for l in range(k + 1, group):
+                across[l] = across[l] - column * (across[l][i : i + 1, :] * inv)
+            both = both - column * scaled
+    inverse = both[:, width:] * jnp.sqrt(diag[:, :width])
     rows = dot3(two(inverse), two(aug[lo : lo + width, :]))
     linv[lo : lo + width, :] = rows[:, n:]
     if lo + width < n:
@@ -71,10 +83,10 @@
 
 
 def kernel(
-    nrow, ncol, chunks, width,
+    nrow, ncol, chunks, skew, width,
     x, pivots, sketch,
     perm_hbm, w_high, w_low, s_high, s_low, upper_out, sketch_out,
-    onehot, picked, moved_in, from_left, from_right, to_right, to_left,
+    picked, moved_in, from_left, from_right, to_right, to_left,
     panel, perm, product, summed, core_in, reduce_in, totals, gram, gram_in, gram_parts, aug, linv,
     sk_pad, sk_pick, sk_in, sk_part, sk_all,
     zr_s, zr_r, zl_s, zl_r, g1, g2_s, g2_r, g3, c_s, c_r, r_s, r_r, a_s, a_r, f_s, f_r, out_sem,
@@ -158,31 +170,26 @@
     mine = (local >= 0) & (local < columns)
     before = local < 0
 
+    pl.semaphore_wait(barrier, nrow + ncol - 2)
+
+    @pl.loop(1, nrow)
+    def _(d):
+        sk_reduce(d).start()
+
+    former_hot = jnp.where(iota((n, n), 0) == partner, 1.0, 0.0).astype(bf16)
+    size = rows // chunks
+
+    picked[...] = jnp.zeros_like(picked)
+
     @pl.loop(0, tiles)
     def _(t):
         at = pl.multiple_of(t * n, n)
-        onehot[pl.ds(at, n), :] = jnp.where(iota((n, n), 0) + at == local, 1.0, 0.0).astype(bf16)
-
-    pl.semaphore_wait(barrier, nrow + ncol - 2)
-
-    @pl.loop(1, nrow)
-    def _(d):
-        sk_reduce(d).start()
-
-    former_hot = jnp.where(iota((n, n), 0) == partner, 1.0, 0.0).astype(bf16)
-    size = rows // chunks
-
-    @pl.loop(0, chunks)
-    def _(c):
-        at = pl.ds(pl.multiple_of(c * size, size), size)
-        picked[at, :] = pick3(three(x[at, :]), onehot[...])
+        onehot = jnp.where(iota((n, n), 0) + at == local, 1.0, 0.0).astype(bf16)
+        picked[...] += pick3(three(x[:, pl.ds(at, n)]), onehot)
 
     @pl.when(z == 0)
     def _():
-        @pl.loop(0, chunks)
-        def _(c):
-            at = pl.ds(pl.multiple_of(c * size, size), size)
-            moved_in[at, :] = pick3(three(x[at, :n]), former_hot)
+        moved_in[...] = pick3(three(x[:, :n]), former_hot)
 
     def right(c):
         at = pl.ds(pl.multiple_of(c * size, size), size)
@@ -192,9 +199,9 @@
         at = pl.ds(pl.multiple_of(c * size, size), size)
         return remote(to_left.at[at, :], from_right.at[at, :], zl_s.at[c], zl_r.at[c], {"col": z - 1})
 
-    @pl.loop(0, chunks + ncol - 1)
+    @pl.loop(0, chunks + skew * (ncol - 1))
     def _(t):
-        c = t - z
+        c = t - skew * z
 
         @pl.when((c >= 0) & (c < chunks))
         def _():
@@ -210,7 +217,7 @@
                 to_right[at, :] = jnp.where(mine, picked[at, :], moved_in[at, :])
                 right(c).start()
 
-        e = t - (ncol - 1 - z)
+        e = t - skew * (ncol - 1 - z)
 
         @pl.when((e >= 0) & (e < chunks))
         def _():
@@ -419,7 +426,12 @@
         out_copy(t).wait()
 
 
-def project(perm, w_high, w_low, s_high, s_low, out):
+def project(perm, w_high, w_low, s_high, s_low, upper, sketch, out, upper_out, sketch_out):
+    @pl.when(pl.program_id(0) == 0)
+    def _():
+        upper_out[...] = upper[...]
+        sketch_out[...] = sketch[...]
+
     out[...] = perm[...] - dot3((w_high[...], w_low[...]), (s_high[...], s_low[...]))
 
 
@@ -428,7 +440,8 @@
     n = pivots.shape[0]
     sk, pieces = sketch.shape
     padded = (sk + 127) // 128 * 128
-    chunks = 10
+    chunks = 20
+    skew = 3
     width = 64
     chips = nrow // 2
     share = columns // nrow
@@ -438,7 +451,7 @@
     dma = pltpu.SemaphoreType.DMA
     shape = jax.ShapeDtypeStruct
     perm, w_high, w_low, s_high, s_low, upper, new_sketch = pl.pallas_call(
-        functools.partial(kernel, nrow, ncol, chunks, width),
+        functools.partial(kernel, nrow, ncol, chunks, skew, width),
         out_shape=[
             shape((rows, columns), f32),
             shape((rows, n), bf16),
@@ -451,7 +464,6 @@
         in_specs=[vmem] * 3,
         out_specs=[pl.BlockSpec(memory_space=pl.ANY)] + [vmem] * 6,
         scratch_shapes=[
-            pltpu.VMEM((columns, n), bf16),
             full, full, full, full, full, full, full,
             pltpu.VMEM((rows, columns), f32),
             pltpu.VMEM((columns, n), f32),
@@ -488,14 +500,16 @@
     tile = 2 * n
     whole = pl.BlockSpec((rows, n), lambda i: (0, 0))
     across = pl.BlockSpec((n, tile), lambda i: (0, i))
-    trailing = pl.pallas_call(
+    small = [pl.BlockSpec(a.shape, lambda i: (0, 0)) for a in (upper, new_sketch)]
+    trailing, upper, new_sketch = pl.pallas_call(
         project,
         grid=(columns // tile,),
-        out_shape=jax.ShapeDtypeStruct((rows, columns), f32),
-        in_specs=[pl.BlockSpec((rows, tile), lambda i: (0, i)), whole, whole, across, across],
-        out_specs=pl.BlockSpec((rows, tile), lambda i: (0, i)),
+        out_shape=[shape((rows, columns), f32), shape(upper.shape, f32), shape(new_sketch.shape, f32)],
+        in_specs=[pl.BlockSpec((rows, tile), lambda i: (0, i)), whole, whole, across, across]
+        + small,
+        out_specs=[pl.BlockSpec((rows, tile), lambda i: (0, i))] + small,
         compiler_params=pltpu.CompilerParams(vmem_limit_bytes=56 * 1024 * 1024),
-    )(perm, w_high, w_low, s_high, s_low)
+    )(perm, w_high, w_low, s_high, s_low, upper, new_sketch)
     return (upper, trailing, new_sketch)
 
 

time: 116 us -> 99.8 us (0.86)
  Pallas kernels: 114 us -> 99 us
  local copies, waits for them, and re-layouts: 1.42 us -> 0 us
    pallas_call x2, Pallas kernels: 114 us -> 99 us  [the longest x1 91.5 us: per_device(): pl.pallas_call(functools.partial(kernel, nrow, ncol, chunks, skew, width)...]
    unnamed x6 -> x0, local copies, waits for them, and re-layouts: 1.42 us -> none
where the time goes in v3:
time: 99.8 us; the launch traced here: 99.6 us
  Pallas kernels  99 us (99%)
    pallas_call x1, Pallas kernels, per_device(): pl.pallas_call(functools.partial(kernel, nrow, ncol, chunks, skew, width)...  91.5 us
    pallas_call x1, Pallas kernels, per_device(): pl.pallas_call(project, grid=(columns // tile,), out_shape=[shape((rows,...  7.47 us

profile of v3, /device:TPU:0, one launch (start us, length us, event | category | flops | bytes accessed | tf_op | source)
XLA Modules:
  0.0 99.6 jit_solution(164374932903973039)
XLA Ops:
  0.6 91.5 %shard_map.58 = (f32[640,2048]{1,0:T(8,128)}, bf16[640,256]{1,0:T(8,128)(2,1)}, bf16[640,256]{1,0:T(8,128)(2,1)}, bf16[256,2048]{1,0:T(8,128)(2,1)}, bf16[256,20...) custom-call(f32[640,2048]{1,0:T(8,128)} %x.1, s32[1,256]{1,0:T(1,128)} %bitcast.1, f32[264,256]{1,0:T(8,128)} %sketch.1), custom_call_target="tpu_custom_call" | custom-call | flops 6710886400 | bytes 10485760 | tf_op jit(solution)/shard_map/pallas_call | solution.py:453
  92.1 7.5 %shard_map.59 = (f32[640,2048]{1,0:T(8,128)}, f32[256,256]{1,0:T(8,128)}, f32[264,256]{1,0:T(8,128)}) custom-call(f32[640,2048]{1,0:T(8,128)} %get-tuple-element.13.perm, bf16[640,256]{1,0:T(8,128)(2,1)} %get-tuple-element.14.w_high, bf16[640,256]{1,0:T(8,128)(2,1)} %get-tuple-element.15.w_low, bf16[256,2048]{1,0:T(8,128)(2,1)} %get-tuple-element.16.s_high, ...), custom_call_target="tpu_custom_call" | custom-call | tf_op jit(solution)/shard_map/pallas_call | solution.py:504

commit v4 on v3

--- a/solution.py
+++ b/solution.py
@@ -90,7 +90,7 @@
     panel, perm, product, summed, core_in, reduce_in, totals, gram, gram_in, gram_parts, aug, linv,
     sk_pad, sk_pick, sk_in, sk_part, sk_all,
     zr_s, zr_r, zl_s, zl_r, g1, g2_s, g2_r, g3, c_s, c_r, r_s, r_r, a_s, a_r, f_s, f_r, out_sem,
-    ks_s, ks_r, kz_s, kz_r, ka_s, ka_r, kf_s, kf_r,
+    gz_s, gz_r, ks_s, ks_r, kz_s, kz_r, ka_s, ka_r, kf_s, kf_r,
 ):
     rows, columns = x.shape
     n = panel.shape[1]
@@ -253,20 +253,70 @@
     first.wait()
     mine_rows = pl.ds(pl.multiple_of(core * half, half), half)
     other_rows = pl.ds(pl.multiple_of((1 - core) * half, half), half)
-    gram_parts[0, :, :] = gram[mine_rows, :] + gram_in[mine_rows, :]
+    quarter = half // ncol
+
+    def gram_rows(place):
+        return pl.ds(pl.multiple_of(core * half + place * quarter, quarter), quarter)
+
+    gram_parts[0, :, :] = gram[gram_rows(z), :] + gram_in[gram_rows(z), :]
+    aug[:, n:] = jnp.where(iota((n, n), 0) == iota((n, n), 1), 1.0, 0.0).astype(f32)
 
     def gram_to(d):
         return remote(gram_parts.at[0], gram_parts.at[d], g2_s.at[d], g2_r.at[d], {"row": peer(d)})
 
     for d in range(1, chips):
         gram_to(d).start()
+
+    def gram_along(d, place):
+        at = gram_rows(place)
+        return remote(aug.at[at, :n], aug.at[at, :n], gz_s.at[d], gz_r.at[d], along(d))
+
+    last = remote(aug.at[mine_rows, :n], aug.at[mine_rows, :n], g3.at[0], g3.at[1], {"row": mate})
+
+    def gram_over_chips():
+        for d in range(1, chips):
+            gram_to(d).wait()
+        total = jnp.zeros((quarter, n), f32)
+        for d in range(chips):
+            total = total + gram_parts[lax.rem(chip + chips - d, chips), :, :]
+        aug[gram_rows(z), :n] = total
+        for d in range(1, ncol):
+            gram_along(d, z).start()
+
+    def gram_over_line():
+        for d in range(1, ncol):
+            gram_along(d, z).wait_send()
+            gram_along(d, lax.rem(z + ncol - d, ncol)).wait_recv()
+        last.start()
 
     def out_copy(t):
         at = pl.ds(pl.multiple_of(t * n, n), n)
         return pltpu.make_async_copy(perm.at[:, at], perm_hbm.at[:, at], out_sem.at[t])
 
+    def part(owner):
+        return pl.ds(pl.multiple_of(owner * share, share), share)
+
+    def to_mate(c):
+        return remote(product.at[part(2 * c + 1 - core), :], core_in.at[c], c_s.at[c], c_r.at[c], {"row": mate})
+
+    def reduce_to(d):
+        return remote(totals.at[lax.rem(chip + d, chips)], reduce_in.at[d], r_s.at[d], r_r.at[d], {"row": peer(d)})
+
+    def add_cores(c):
+        to_mate(c).wait()
+        totals[c, :, :] = product[part(2 * c + core), :] + core_in[c, :, :]
+
+    def send_sums(d):
+        add_cores(lax.rem(chip + d, chips))
+        reduce_to(d).start()
+
+    per_tile = n // share
+    per_chip = 2 * share // n
+    begin = lax.rem(chip + 1, chips) * 2 * share // n
+
     @pl.loop(0, tiles)
-    def _(t):
+    def _(u):
+        t = lax.rem(begin + u, tiles)
         at = pl.multiple_of(t * n, n)
         place = (iota((n, n), 1) + at == wanted) & usable
         place = jnp.where(place, 1.0, 0.0)
@@ -277,24 +327,32 @@
         out_copy(t).start()
         product[pl.ds(at, n), :] = dot3(left_parts, two(tile)).T
 
-    def part(owner):
-        return pl.ds(pl.multiple_of(owner * share, share), share)
-
-    def to_mate(c):
-        return remote(product.at[part(2 * c + 1 - core), :], core_in.at[c], c_s.at[c], c_r.at[c], {"row": mate})
-
-    for c in range(chips):
-        to_mate(c).start()
-
-    for c in range(chips):
-        to_mate(c).wait()
-        totals[c, :, :] = product[part(2 * c + core), :] + core_in[c, :, :]
-
-    def reduce_to(d):
-        return remote(totals.at[lax.rem(chip + d, chips)], reduce_in.at[d], r_s.at[d], r_r.at[d], {"row": peer(d)})
-
-    for d in range(1, chips):
-        reduce_to(d).start()
+        for i in range(per_tile):
+            owner = t * per_tile + i
+
+            @pl.when(lax.rem(owner, 2) != core)
+            def _():
+                to_mate(owner // 2).start()
+
+        if per_chip > 0:
+            ready = (u + 1) // per_chip
+
+            @pl.when((lax.rem(u + 1, per_chip) == 0) & (ready >= 2))
+            def _():
+                send_sums(ready - 1)
+
+        @pl.when(u == tiles // 2)
+        def _():
+            gram_over_chips()
+
+        @pl.when(u == tiles - 1)
+        def _():
+            gram_over_line()
+
+    if per_chip == 0:
+        for d in range(1, chips):
+            send_sums(d)
+    add_cores(chip)
 
     @pl.loop(1, nrow)
     def _(d):
@@ -304,15 +362,6 @@
     for d in range(1, ncol):
         sk_along(d).start()
 
-    for d in range(1, chips):
-        gram_to(d).wait()
-    gram_half = jnp.zeros((half, n), f32)
-    for d in range(chips):
-        gram_half = gram_half + gram_parts[lax.rem(chip + chips - d, chips), :, :]
-    aug[mine_rows, :n] = gram_half
-    last = remote(aug.at[mine_rows, :n], aug.at[mine_rows, :n], g3.at[0], g3.at[1], {"row": mate})
-    last.start()
-    aug[:, n:] = jnp.where(iota((n, n), 0) == iota((n, n), 1), 1.0, 0.0).astype(f32)
     last.wait_send()
     remote(aug.at[other_rows, :n], aug.at[other_rows, :n], g3.at[0], g3.at[1], {"row": mate}).wait_recv()
 
@@ -473,7 +522,7 @@
             pltpu.VMEM((chips, share, n), f32),
             pltpu.VMEM((n, n), f32),
             pltpu.VMEM((n, n), f32),
-            pltpu.VMEM((chips, n // 2, n), f32),
+            pltpu.VMEM((chips, n // 2 // ncol, n), f32),
             pltpu.VMEM((n, 2 * n), f32),
             pltpu.VMEM((n, n), f32),
             pltpu.VMEM((padded, pieces), f32),
@@ -486,6 +535,7 @@
             dma((chips,)), dma((chips,)), dma((chips,)), dma((chips,)),
             dma((chips,)), dma((chips,)), dma((chips,)), dma((chips,)),
             dma((columns // n,)),
+            dma((ncol,)), dma((ncol,)),
             dma((nrow,)), dma((nrow,)), dma((ncol,)), dma((ncol,)),
             dma((chips,)), dma((chips,)), dma((chips,)), dma((chips,)),
         ],

time: 99.8 us -> 95 us (0.952)
  Pallas kernels: 99 us -> 94.2 us
    pallas_call x1, Pallas kernels: 91.5 us -> 86.7 us  [per_device(): pl.pallas_call(functools.partial(kernel, nrow, ncol, chunks, skew, width)...]
where the time goes in v4:
time: 95 us; the launch traced here: 94.8 us
  Pallas kernels  94.2 us (99%)
    pallas_call x1, Pallas kernels, per_device(): pl.pallas_call(functools.partial(kernel, nrow, ncol, chunks, skew, width)...  86.7 us
    pallas_call x1, Pallas kernels, per_device(): pl.pallas_call(project, grid=(columns // tile,), out_shape=[shape((rows,...  7.47 us

profile of v4, /device:TPU:0, one launch (start us, length us, event | category | flops | bytes accessed | tf_op | source)
XLA Modules:
  0.0 94.8 jit_solution(2558676350154936826)
XLA Ops:
  0.6 86.7 %shard_map.58 = (f32[640,2048]{1,0:T(8,128)}, bf16[640,256]{1,0:T(8,128)(2,1)}, bf16[640,256]{1,0:T(8,128)(2,1)}, bf16[256,2048]{1,0:T(8,128)(2,1)}, bf16[256,20...) custom-call(f32[640,2048]{1,0:T(8,128)} %x.1, s32[1,256]{1,0:T(1,128)} %bitcast.1, f32[264,256]{1,0:T(8,128)} %sketch.1), custom_call_target="tpu_custom_call" | custom-call | flops 6710886400 | bytes 10485760 | tf_op jit(solution)/shard_map/pallas_call | solution.py:502
  87.3 7.5 %shard_map.59 = (f32[640,2048]{1,0:T(8,128)}, f32[256,256]{1,0:T(8,128)}, f32[264,256]{1,0:T(8,128)}) custom-call(f32[640,2048]{1,0:T(8,128)} %get-tuple-element.13.perm, bf16[640,256]{1,0:T(8,128)(2,1)} %get-tuple-element.14.w_high, bf16[640,256]{1,0:T(8,128)(2,1)} %get-tuple-element.15.w_low, bf16[256,2048]{1,0:T(8,128)(2,1)} %get-tuple-element.16.s_high, ...), custom_call_target="tpu_custom_call" | custom-call | tf_op jit(solution)/shard_map/pallas_call | solution.py:554

commit v5 on v4

--- a/solution.py
+++ b/solution.py
@@ -405,6 +405,8 @@
         for d in range(1, chips):
             gather_to(d).start()
         forward(0).start()
+
+    def finish_sketch():
         for d in range(1, ncol):
             sk_along(d).wait()
         sk_all[slots_of(me), :] = jnp.sum(sk_part[...], axis=0)
@@ -420,8 +422,10 @@
     blocks = n // width
     for b in range(blocks):
         cholesky_block(aug, linv, b, width)
+        if b == 0:
+            finish_reduce()
         if b == blocks // 2 - 1:
-            finish_reduce()
+            finish_sketch()
     finish_gather()
     for d in range(1, chips):
         sk_gathered(d).wait_recv()

time: 95 us -> 95 us (level)
  no operation moved by 1% of the time
where the time goes in v5:
time: 95 us; the launch traced here: 94.8 us
  Pallas kernels  94.2 us (99%)
    pallas_call x1, Pallas kernels, per_device(): pl.pallas_call(functools.partial(kernel, nrow, ncol, chunks, skew, width)...  86.7 us
    pallas_call x1, Pallas kernels, per_device(): pl.pallas_call(project, grid=(columns // tile,), out_shape=[shape((rows,...  7.47 us

profile of v5, /device:TPU:0, one launch (start us, length us, event | category | flops | bytes accessed | tf_op | source)
XLA Modules:
  0.0 94.8 jit_solution(2947694723554819243)
XLA Ops:
  0.6 86.7 %shard_map.58 = (f32[640,2048]{1,0:T(8,128)}, bf16[640,256]{1,0:T(8,128)(2,1)}, bf16[640,256]{1,0:T(8,128)(2,1)}, bf16[256,2048]{1,0:T(8,128)(2,1)}, bf16[256,20...) custom-call(f32[640,2048]{1,0:T(8,128)} %x.1, s32[1,256]{1,0:T(1,128)} %bitcast.1, f32[264,256]{1,0:T(8,128)} %sketch.1), custom_call_target="tpu_custom_call" | custom-call | flops 6710886400 | bytes 10485760 | tf_op jit(solution)/shard_map/pallas_call | solution.py:506
  87.3 7.5 %shard_map.59 = (f32[640,2048]{1,0:T(8,128)}, f32[256,256]{1,0:T(8,128)}, f32[264,256]{1,0:T(8,128)}) custom-call(f32[640,2048]{1,0:T(8,128)} %get-tuple-element.13.perm, bf16[640,256]{1,0:T(8,128)(2,1)} %get-tuple-element.14.w_high, bf16[640,256]{1,0:T(8,128)(2,1)} %get-tuple-element.15.w_low, bf16[256,2048]{1,0:T(8,128)(2,1)} %get-tuple-element.16.s_high, ...), custom_call_target="tpu_custom_call" | custom-call | tf_op jit(solution)/shard_map/pallas_call | solution.py:558

commit v6 on v4

--- a/solution.py
+++ b/solution.py
@@ -56,22 +56,27 @@
     lo = b * width
     eye = jnp.where(iota((width, width), 0) == iota((width, width), 1), 1.0, 0.0).astype(f32)
     both = jnp.concatenate([aug[lo : lo + width, lo : lo + width], eye], axis=1)
-    below = iota((width, 2 * width), 0)
-    diag = jnp.ones((width, 2 * width), f32)
-    group = 4
+    group = 8
+    done, scales = [], []
     for first in range(0, width, group):
+        below = iota(both.shape, 0)
         across = [
             jnp.broadcast_to(both[:, i : i + 1], both.shape) for i in range(first, first + group)
         ]
+        scale = jnp.ones((group, 2 * width), f32)
         for k in range(group):
-            i = first + k
-            inv = 1.0 / across[k][i : i + 1, :]
-            diag = jnp.where(below == i, inv, diag)
-            scaled = both[i : i + 1, :] * inv
-            column = jnp.where(below > i, across[k], 0.0)
+            inv = 1.0 / across[k][k : k + 1, :]
+            scale = jnp.where(below[:group, :] == k, inv, scale)
+            scaled = both[k : k + 1, :] * inv
+            column = jnp.where(below > k, across[k], 0.0)
             for l in range(k + 1, group):
-                across[l] = across[l] - column * (across[l][i : i + 1, :] * inv)
+                across[l] = across[l] - column * (across[l][k : k + 1, :] * inv)
             both = both - column * scaled
+        done.append(both[:group, :])
+        scales.append(scale)
+        both = both[group:, :]
+    both = jnp.concatenate(done, axis=0)
+    diag = jnp.concatenate(scales, axis=0)
     inverse = both[:, width:] * jnp.sqrt(diag[:, :width])
     rows = dot3(two(inverse), two(aug[lo : lo + width, :]))
     linv[lo : lo + width, :] = rows[:, n:]

time: 95 us -> 95 us (level)
  no operation moved by 1% of the time
where the time goes in v6:
time: 95 us; the launch traced here: 94.8 us
  Pallas kernels  94.2 us (99%)
    pallas_call x1, Pallas kernels, per_device(): pl.pallas_call(functools.partial(kernel, nrow, ncol, chunks, skew, width)...  86.7 us
    pallas_call x1, Pallas kernels, per_device(): pl.pallas_call(project, grid=(columns // tile,), out_shape=[shape((rows,...  7.47 us

profile of v6, /device:TPU:0, one launch (start us, length us, event | category | flops | bytes accessed | tf_op | source)
XLA Modules:
  0.0 94.8 jit_solution(15920087493114543827)
XLA Ops:
  0.6 86.7 %shard_map.58 = (f32[640,2048]{1,0:T(8,128)}, bf16[640,256]{1,0:T(8,128)(2,1)}, bf16[640,256]{1,0:T(8,128)(2,1)}, bf16[256,2048]{1,0:T(8,128)(2,1)}, bf16[256,20...) custom-call(f32[640,2048]{1,0:T(8,128)} %x.1, s32[1,256]{1,0:T(1,128)} %bitcast.1, f32[264,256]{1,0:T(8,128)} %sketch.1), custom_call_target="tpu_custom_call" | custom-call | flops 6710886400 | bytes 10485760 | tf_op jit(solution)/shard_map/pallas_call | solution.py:507
  87.3 7.5 %shard_map.59 = (f32[640,2048]{1,0:T(8,128)}, f32[256,256]{1,0:T(8,128)}, f32[264,256]{1,0:T(8,128)}) custom-call(f32[640,2048]{1,0:T(8,128)} %get-tuple-element.13.perm, bf16[640,256]{1,0:T(8,128)(2,1)} %get-tuple-element.14.w_high, bf16[640,256]{1,0:T(8,128)(2,1)} %get-tuple-element.15.w_low, bf16[256,2048]{1,0:T(8,128)(2,1)} %get-tuple-element.16.s_high, ...), custom_call_target="tpu_custom_call" | custom-call | tf_op jit(solution)/shard_map/pallas_call | solution.py:559
